TPU v7x, 32 devices: a whole 2x2x4 slice. The times are simulated.
32 devices in a mesh: chan: 8 (over z, y), state: 4 (over x, core).
Axes of the slice: x: 2, y: 2, z: 4, core: 2. Of those that a mesh axis runs over, the one named last changes fastest.
Arguments:
- hidden_in: float32 [2048, 2048], P('chan'), may hold values from -6 to 6
- norm_gain: float32 [2048], replicated, may hold values from 0.25 to 1.75
- in_weight: bfloat16 [2048, 2, 4096], P(None, None, 'chan'), may hold values from -0.125 to 0.125
- conv_kernel: float32 [4, 4096], P(None, 'chan'), may hold values from -3 to 3
- conv_offset: float32 [4096], P('chan'), may hold values from -3 to 3
- select_rank: bfloat16 [4096, 128], P('chan'), may hold values from -0.09375 to 0.09375
- select_entry: bfloat16 [4096, 16], P('chan', 'state'), may hold values from -0.1875 to 0.1875
- select_read: bfloat16 [4096, 16], P('chan', 'state'), may hold values from -0.1875 to 0.1875
- delta_weight: bfloat16 [128, 4096], P(None, 'chan'), may hold values from -0.5 to 0.5
- step_bias: float32 [4096], P('chan'), as said below
- decay_log: float32 [16, 4096], P('state', 'chan'), may hold values from 0 to 2.77
- skip_weight: float32 [4096], P('chan'), may hold values from 0.5 to 1.5
- out_weight: bfloat16 [4096, 2048], P('chan'), may hold values from -0.375 to 0.375
- lengths: int32 [8], replicated, may hold values from 1 to 1024, 2048 in all
- pad_mask: int32 [2048], replicated, may hold values 0 or 1
- cotangent: float32 [2048, 2048], P('chan'), may hold values from -6 to 6
Outputs:
- result: float32 [2048, 2048], P('chan')
- input_grad: float32 [2048, 2048], P('chan')
- gain_grad: float32 [2048], replicated
- in_grad: float32 [2048, 2, 4096], P(None, None, 'chan')
- kernel_grad: float32 [4, 4096], P(None, 'chan')
- offset_grad: float32 [4096], P('chan')
- rank_grad: float32 [4096, 128], P('chan')
- entry_grad: float32 [4096, 16], P('chan', 'state')
- read_grad: float32 [4096, 16], P('chan', 'state')
- delta_grad: float32 [128, 4096], P(None, 'chan')
- bias_grad: float32 [4096], P('chan')
- decay_grad: float32 [16, 4096], P('state', 'chan')
- skip_grad: float32 [4096], P('chan')
- out_grad: float32 [4096, 2048], P('chan')
Inputs may be any that keep to these rules, and one draw needn't show every extreme that they name: lengths of the 8 sequences packed in order into all 2048 tokens; they sum to 2048 and the longest has exactly 1024. `pad_mask`: 1 marks a real token, 0 padding. `step_bias`: the step-size bias of each inner channel.
All inputs are finite; a program needn't handle non-finite values.
Results may differ from a plain program's by a relative error of at most 0.011.
Values may be sent and summed in bfloat16 or wider, within the bound.
No kernel may reach another device: no remote copies, remote signals or barrier semaphores. Data moves between devices by JAX's collectives and lax.ppermute only.
A program may use at most 384 MiB of HBM per device.

v0:
```python
import jax
import jax.numpy as jnp
from jax import lax
from jax.sharding import PartitionSpec as P

epsilon = 1e-05


def positions(lengths, tokens_all):
    ends = jnp.cumsum(lengths)
    begins = ends - lengths
    places = jnp.arange(tokens_all, dtype=jnp.int32)
    opening = jnp.max(jnp.where(begins[:, None] <= places[None, :], begins[:, None], 0), axis=0)
    return places - opening


def delayed(values, amount):
    if amount == 0:
        return values
    padding = jnp.zeros((amount,) + values.shape[1:], values.dtype)
    return jnp.concatenate([padding, values[: values.shape[0] - amount]], axis=0)


def advanced(values, amount):
    if amount == 0:
        return values
    padding = jnp.zeros((amount,) + values.shape[1:], values.dtype)
    return jnp.concatenate([values[amount:], padding], axis=0)


def silu_slope(values):
    logistic = jax.nn.sigmoid(values)
    return logistic * (1.0 + values * (1.0 - logistic))


def linear_scan(decays, drive):
    total_rows = decays.shape[0]
    blocks = total_rows // 16
    factors = jnp.swapaxes(decays.reshape((blocks, 16) + decays.shape[1:]), 0, 1)
    sources = jnp.swapaxes(drive.reshape((blocks, 16) + drive.shape[1:]), 0, 1)

    def advance(totals, item):
        state_now, product_now = totals
        factor_now, source_now = item
        state_now = factor_now * state_now + source_now
        product_now = factor_now * product_now
        return ((state_now, product_now), (state_now, product_now))

    initial = (jnp.zeros(factors.shape[1:], jnp.float32), jnp.ones(factors.shape[1:], jnp.float32))
    final_pair, (local_states, products) = lax.scan(advance, initial, (factors, sources))

    def combine(early, later):
        return (early[0] * later[0], later[0] * early[1] + later[1])

    joined_factor, joined_state = lax.associative_scan(
        combine, (products[-1], local_states[-1]), axis=0
    )
    entering = jnp.concatenate([jnp.zeros_like(joined_state[:1]), joined_state[:-1]], axis=0)
    states = local_states + products * entering[None]
    return jnp.swapaxes(states, 0, 1).reshape(decays.shape)


def shards(
    hidden_in,
    norm_gain,
    in_weight,
    conv_kernel,
    conv_offset,
    select_rank,
    select_entry,
    select_read,
    delta_weight,
    step_bias,
    decay_log,
    skip_weight,
    out_weight,
    lengths,
    pad_mask,
    cotangent,
):
    rows_dev, width = hidden_in.shape
    tokens_all = pad_mask.shape[0]
    chans = in_weight.shape[2]
    kernel_len = conv_kernel.shape[0]
    per_state = select_entry.shape[1]
    contract_rows = (((0,), (0,)), ((), ()))
    contract_cols = (((1,), (1,)), ((), ()))
    place = positions(lengths, tokens_all)
    fresh = (place > 0).astype(jnp.float32)
    maskf = pad_mask.astype(jnp.float32)[:, None]
    square = jnp.mean(hidden_in * hidden_in, axis=1, keepdims=True)
    inv_rms = lax.rsqrt(square + epsilon)
    scaled = hidden_in * inv_rms
    normed = (scaled * norm_gain[None, :]).astype(jnp.bfloat16)
    in_flat = in_weight.reshape(width, 2 * chans)
    both = jnp.dot(
        lax.all_gather(normed, "chan", axis=0, tiled=True),
        in_flat,
        preferred_element_type=jnp.float32,
    )
    inner = both[:, :chans] * maskf
    gate_in = both[:, chans:]
    valids = []
    shifted = []
    conv = jnp.zeros((tokens_all, chans), jnp.float32) + conv_offset[None, :]
    for index in range(kernel_len):
        lag = kernel_len - 1 - index
        valids.append((place >= lag).astype(jnp.float32)[:, None])
        shifted.append(delayed(inner, lag))
        conv = conv + conv_kernel[index][None, :] * shifted[index] * valids[index]
    act = (jax.nn.silu(conv) * maskf).astype(jnp.bfloat16)
    act_wide = act.astype(jnp.float32)
    pair_map = jnp.concatenate([select_entry, select_read], axis=1)
    rank_part = jnp.dot(act, select_rank, preferred_element_type=jnp.float32)
    pair_part = jnp.dot(act, pair_map, preferred_element_type=jnp.float32)
    raw_sum, pair_sum = lax.psum((rank_part, pair_part), "chan")
    entry = pair_sum[:, :per_state]
    readout = pair_sum[:, per_state:]
    lowrank = raw_sum.astype(jnp.bfloat16)
    dpre = jnp.dot(lowrank, delta_weight, preferred_element_type=jnp.float32) + step_bias[None, :]
    delta = jax.nn.softplus(dpre)
    coeff = -jnp.exp(decay_log)
    decays = jnp.exp(delta[:, None, :] * coeff[None]) * fresh[:, None, None]
    drive = (delta * act_wide)[:, None, :] * entry[:, :, None]
    states = linear_scan(decays, drive)
    scan_part = jnp.sum(readout[:, :, None] * states, axis=1)
    scanned = lax.psum(scan_part, "state")
    mixed = scanned + skip_weight[None, :] * act_wide
    gate_act = jax.nn.silu(gate_in)
    gated = (mixed * gate_act).astype(jnp.bfloat16)
    gated_rows = gated
    branch = lax.psum_scatter(
        jnp.dot(gated_rows, out_weight, preferred_element_type=jnp.float32),
        "chan",
        scatter_dimension=0,
        tiled=True,
    )
    result = hidden_in + branch
    grad_low = cotangent.astype(jnp.bfloat16)
    pieces = lax.all_gather(grad_low, "chan", axis=0, tiled=True)
    gated_rows = gated
    product = lax.dot_general(pieces, out_weight, contract_cols, preferred_element_type=jnp.float32)
    outw_acc = lax.dot_general(
        gated_rows, pieces, contract_rows, preferred_element_type=jnp.float32
    )
    dmix = product * gate_act
    dgate = product * mixed * silu_slope(gate_in)
    skip_grad = jnp.sum(dmix * act_wide, axis=0)
    emitted = readout[:, :, None] * dmix[:, None, :]
    following = jnp.concatenate([decays[1:], jnp.zeros_like(decays[:1])], axis=0)
    adjoint = jnp.flip(linear_scan(jnp.flip(following, 0), jnp.flip(emitted, 0)), 0)
    earlier = jnp.concatenate([jnp.zeros_like(states[:1]), states[:-1]], axis=0)
    flow = adjoint * earlier * decays
    dread_part = jnp.sum(states * dmix[:, None, :], axis=2)
    dentry_part = jnp.sum(adjoint * (delta * act_wide)[:, None, :], axis=2)
    ddelta_part = jnp.sum(
        flow * coeff[None] + adjoint * entry[:, :, None] * act_wide[:, None, :], axis=1
    )
    decay_grad = coeff * jnp.sum(flow * delta[:, None, :], axis=0)
    dact_scan = jnp.sum(adjoint * entry[:, :, None], axis=1) * delta
    dentry_sum, dread_sum = lax.psum((dentry_part, dread_part), "chan")
    dpair = jnp.concatenate(
        [dentry_sum.astype(jnp.bfloat16), dread_sum.astype(jnp.bfloat16)], axis=1
    )
    pair_grad = lax.dot_general(act, dpair, contract_rows, preferred_element_type=jnp.float32)
    entry_grad = pair_grad[:, :per_state]
    read_grad = pair_grad[:, per_state:]
    dact_pair = lax.dot_general(dpair, pair_map, contract_cols, preferred_element_type=jnp.float32)
    dact_state, ddelta = lax.psum((dact_scan + dact_pair, ddelta_part), "state")
    ddpre = (ddelta * jax.nn.sigmoid(dpre)).astype(jnp.bfloat16)
    bias_grad = jnp.sum(ddpre.astype(jnp.float32), axis=0)
    delta_grad = lax.dot_general(lowrank, ddpre, contract_rows, preferred_element_type=jnp.float32)
    dlow_part = lax.dot_general(
        ddpre, delta_weight, contract_cols, preferred_element_type=jnp.float32
    )
    dlow = lax.psum(dlow_part, "chan").astype(jnp.bfloat16)
    rank_grad = lax.dot_general(act, dlow, contract_rows, preferred_element_type=jnp.float32)
    dact = (
        dact_state
        + dmix * skip_weight[None, :]
        + lax.dot_general(dlow, select_rank, contract_cols, preferred_element_type=jnp.float32)
    )
    dconv = dact * maskf * silu_slope(conv)
    offset_grad = jnp.sum(dconv, axis=0)
    kernel_rows = []
    dinner = jnp.zeros((tokens_all, chans), jnp.float32)
    for index in range(kernel_len):
        lag = kernel_len - 1 - index
        masked = dconv * valids[index]
        kernel_rows.append(jnp.sum(masked * shifted[index], axis=0))
        dinner = dinner + advanced(masked * conv_kernel[index][None, :], lag)
    kernel_grad = jnp.stack(kernel_rows, axis=0)
    dboth = jnp.concatenate([dinner * maskf, dgate], axis=1).astype(jnp.bfloat16)
    chosen = dboth
    in_flat_grad = lax.dot_general(
        lax.all_gather(normed, "chan", axis=0, tiled=True),
        chosen,
        contract_rows,
        preferred_element_type=jnp.float32,
    )
    in_grad = in_flat_grad.reshape(width, 2, chans)
    chosen = dboth
    dnormed = lax.psum_scatter(
        lax.dot_general(chosen, in_flat, contract_cols, preferred_element_type=jnp.float32),
        "chan",
        scatter_dimension=0,
        tiled=True,
    )
    gain_part = jnp.sum(dnormed * scaled, axis=0)
    gain_grad = lax.psum(gain_part, "chan")
    dscaled = dnormed * norm_gain[None, :]
    input_grad = cotangent + inv_rms * (
        dscaled - scaled * jnp.mean(dscaled * scaled, axis=1, keepdims=True)
    )
    return (
        result,
        input_grad,
        gain_grad,
        in_grad,
        kernel_grad,
        offset_grad,
        rank_grad,
        entry_grad,
        read_grad,
        delta_grad,
        bias_grad,
        decay_grad,
        skip_grad,
        outw_acc,
    )


def solution(mesh):
    return jax.shard_map(
        shards,
        mesh=mesh,
        in_specs=(
            P("chan", None),
            P(),
            P(None, None, "chan"),
            P(None, "chan"),
            P("chan"),
            P("chan", None),
            P("chan", "state"),
            P("chan", "state"),
            P(None, "chan"),
            P("chan"),
            P("state", "chan"),
            P("chan"),
            P("chan", None),
            P(),
            P(),
            P("chan", None),
        ),
        out_specs=(
            P("chan", None),
            P("chan", None),
            P(),
            P(None, None, "chan"),
            P(None, "chan"),
            P("chan"),
            P("chan", None),
            P("chan", "state"),
            P("chan", "state"),
            P(None, "chan"),
            P("chan"),
            P("state", "chan"),
            P("chan"),
            P("chan", None),
        ),
        check_vma=False,
    )
```

profile of v0, /device:TPU:0, one launch (start us, length us, event | category | flops | bytes accessed | tf_op | source)
XLA Modules:
  0.0 2468.6 jit_solution(2004236104488265578)
XLA Ops:
  22.2 118.2 %all-gather.3.cloned.1.call-done = bf16[2048,2048]{1,0:T(8,128)(2,1)} async-done(((bf16[256,2048]{1,0:T(8,128)(2,1)}), bf16[2048,2048]{1,0:T(8,128)(2,1)}) %all-gather.3.cloned.1.call-update) | async-done | bytes 8388624 | tf_op jit(solution)/shard_map/all_gather | solution.py:97
  140.4 12.5 fusion.50
  158.6 107.6 %all-gather.5.cloned.1.call-done = bf16[2048,2048]{1,0:T(8,128)(2,1)} async-done(((bf16[256,2048]{1,0:T(8,128)(2,1)}), bf16[2048,2048]{1,0:T(8,128)(2,1)}) %all-gather.5.cloned.1.call-update) | async-done | bytes 8388624 | tf_op jit(solution)/shard_map/all_gather | solution.py:140
  266.4 21.8 multiply_reduce_fusion.3
  291.5 69.9 %all-reduce.51 = bf16[2048,128]{1,0:T(8,128)(2,1)S(1)} all-reduce(f32[2048,128]{1,0:T(8,128)} %fusion.51), channel_id=1, replica_groups=mesh['chan'=8,'state'=4] {'chan'}, use_global_device_ids=true, to_apply=%region_4.5 | all-reduce | flops 262144 | bytes 1572864 | tf_op jit(solution)/shard_map/psum | solution.py:116
  396.5 127.5 %rev.10 = f32[2048,4,512]{2,0,1:T(8,128)} reverse(f32[2048,4,512]{2,0,1:T(8,128)} %concatenate.87), dimensions={0} | reverse | bytes 33554432 | tf_op jit(solution)/shard_map/jit(_flip)/rev | solution.py:151
  545.2 127.6 %rev.11 = f32[2048,4,512]{2,0,1:T(8,128)} reverse(f32[2048,4,512]{2,0,1:T(8,128)} %broadcast_multiply_fusion), dimensions={0} | reverse | bytes 33554432 | tf_op jit(solution)/shard_map/jit(_flip)/rev | solution.py:151
  684.9 228.0 %while.35 = (s32[]{:T(128)}, f32[128,4,512]{2,1,0:T(4,128)}, f32[128,4,512]{2,1,0:T(4,128)}, f32[16,128,4,512]{3,2,1,0:T(4,128)}, f32[16,128,4,512]{3,2,1,0:T(4,...) while((s32[]{:T(128)}, f32[128,4,512]{2,1,0:T(4,128)}, ...), condition=%wide.region_11.12_spmd.clone, body=%wide.region_10.11_spmd.clone.sunk | while | flops 1310723 | bytes 12583531 | solution.py:50
  977.3 15.3 pad.121
  999.1 14.5 exponential_multiply_fusion.1
  1025.9 66.3 %while.34 = (s32[]{:T(128)}, f32[128,4,512]{2,1,0:T(4,128)S(1)}, f32[128,4,512]{2,1,0:T(4,128)}, f32[16,128,4,512]{3,2,1,0:T(4,128)}, f32[16,128,4,512]{3,2,1,0:...) while((s32[]{:T(128)}, f32[128,4,512]{2,1,0:T(4,128)S(1)}, ...), condition=%wide.region_6.7_spmd.clone, body=%wide.region_5.6_spmd.clone.sunk | while | flops 1310723 | bytes 8389223 | solution.py:50
  1149.4 10.5 pad.106
  1159.9 15.3 pad.107
  1180.6 22.8 pad.235
  1205.4 29.7 %pad.162 = f32[127,4,512]{2,1,0:T(4,128)} pad(f32[64,4,512]{2,1,0:T(4,128)} %pad_maximum_fusion.4, f32[]{:T(128)} %constant.26.clone.1), padding=0_0_1x0_0_0x0_0_0 | pad | bytes 1564676 | tf_op jit(solution)/shard_map/slice | solution.py:58
  1237.0 31.7 %copy_add_fusion = f32[16,128,4,512]{3,0,1,2:T(8,128)} fusion(f32[16,128,4,512]{3,2,1,0:T(4,128)} %get-tuple-element.92, f32[16,128,4,512]{3,2,1,0:T(4,128)} %get-tuple-element.93, f32[128,4,512]{2,0,1:T(8,128)S(1)} %concatenate.94.clone), kind=kLoop, calls=%fused_computation.18 | loop fusion | flops 8388608 | bytes 51380224 | tf_op jit(solution)/shard_map/add | solution.py:59
  1268.8 127.5 %rev.12 = f32[2048,4,512]{2,0,1:T(8,128)} reverse(f32[2048,4,512]{2,0,1:T(8,128)} %bitcast.132), dimensions={0} | reverse | bytes 33554432 | tf_op jit(solution)/shard_map/jit(_flip)/rev | solution.py:151
  1396.3 22.8 pad.234
  1421.0 29.7 %pad.160 = f32[127,4,512]{2,1,0:T(4,128)} pad(f32[64,4,512]{2,1,0:T(4,128)} %pad_maximum_fusion.3, f32[]{:T(128)} %constant.26.clone.1), padding=0_0_1x0_0_0x0_0_0 | pad | bytes 1564676 | tf_op jit(solution)/shard_map/slice | solution.py:58
  1453.2 40.9 %fusion.2 = (f32[128,16,4]{1,0,2:T(8,128)S(1)}, f32[128,16,512]{2,1,0:T(8,128)}, f32[16,128,4,512]{3,0,1,2:T(8,128)}) fusion(f32[128,16,512]{2,1,0:T(8,128)S(1)} %bitcast.133, f32[128,16,4]{1,0,2:T(8,128)S(1)} %mul.585, f32[128,4,512]{2,0,1:T(8,128)S(1)} %concatenate.86.clone, f32[16,128,4,512]{3,2,1,0:T(4,128)} %get-tuple-element.91, ...), kind=kLoop, calls=%fused_computation.17 | loop fusion | flops 24109056 | bytes 59834368 | tf_op jit(solution)/shard_map/reduce_sum | solution.py:154
  1494.2 20.9 multiply_reduce_fusion
  1515.3 85.5 %all-reduce.48.cloned.1.call-done = f32[2048,512]{1,0:T(8,128)} async-done(((f32[2048,512]{1,0:T(8,128)}), f32[2048,512]{1,0:T(8,128)}) %all-reduce.48.cloned.1.call-update) | async-done | bytes 4194320 | tf_op jit(solution)/shard_map/psum | solution.py:169
  1608.1 73.0 %all-reduce.52 = (bf16[2048,4]{0,1:T(4,128)(2,1)S(1)}, bf16[2048,4]{0,1:T(4,128)(2,1)S(1)}, bf16[2048,128]{1,0:T(8,128)(2,1)}) all-reduce(f32[2048,4]{0,1:T(4,128)S(1)} %reduce_sum.154, f32[2048,4]{0,1:T(4,128)S(1)} %get-tuple-element.243, f32[2048,128]{1,0:T(8,128)S(1)} %fusion.53), channel_id=1, replica_groups=mesh['chan'=8,'state'=4] {'chan'}, use_global_device_ids=true, to_apply=%region_16.17 | all-reduce | flops 278528 | bytes 1671168 | tf_op jit(solution)/shard_map/psum | solution.py:161
  1687.5 151.4 %all-reduce.50.cloned.1.call-done = (f32[2048,512]{1,0:T(8,128)}, f32[2048,512]{1,0:T(8,128)}) async-done(((f32[2048,512]{1,0:T(8,128)}, f32[2048,512]{1,0:T(8,128)}), (f32[2048,512]{1,0:T(8,128)}, f32[2048,512]{1,0:T(8,128)})) %all-reduce.50.cloned.1.call-update) | async-done | bytes 8388624 | tf_op jit(solution)/shard_map/psum | solution.py:127
  1838.9 14.5 multiply_reduce_fusion.7
  1871.3 15.1 fusion.5
  1905.1 13.7 fusion.4
  1918.7 13.5 copy.89
  1932.9 10.7 fusion.54
  1943.5 226.0 %reduce-scatter.5.cloned.1.call-done = f32[256,2048]{1,0:T(8,128)} async-done(((f32[2048,2048]{1,0:T(8,128)}), f32[256,2048]{1,0:T(8,128)}) %reduce-scatter.5.cloned.1.call-update) | async-done | bytes 2097168 | tf_op jit(solution)/shard_map/reduce_scatter | solution.py:203
  2172.4 21.0 psum.71
  2193.4 262.0 %reduce-scatter.3.cloned.1.call-done = f32[256,2048]{1,0:T(8,128)} async-done(((f32[2048,2048]{1,0:T(8,128)}), f32[256,2048]{1,0:T(8,128)}) %reduce-scatter.3.cloned.1.call-update) | async-done | bytes 2097168 | tf_op jit(solution)/shard_map/reduce_scatter | solution.py:132
  (369 shorter events, 600.1 us)
Async XLA Ops:
  7.2 259.1 %copy-start = (bf16[512,2048]{1,0:T(8,128)(2,1)S(1)}, bf16[512,2048]{1,0:T(8,128)(2,1)}, u32[]{:S(2)}) copy-start(bf16[512,2048]{1,0:T(8,128)(2,1)} %param.32) | copy-start | bytes 6291460
  7.2 133.2 %all-gather.3.cloned.1.call-start = ((), (), s32[]{:S(2)}) async-start(), calls=%async_computation.2 | async-start | bytes 9437184 | tf_op jit(solution)/shard_map/all_gather | solution.py:97
  12.6 253.6 %all-gather.5.cloned.1.call-start = ((), (), s32[]{:S(2)}) async-start(), calls=%async_computation.5 | async-start | bytes 9437184 | tf_op jit(solution)/shard_map/all_gather | solution.py:140
  15.4 519.8 %all-reduce.46.cloned.1.call-start = ((), (), s32[]{:S(2)}) async-start(), calls=%async_computation.3 | async-start | bytes 131072 | tf_op jit(solution)/shard_map/psum | solution.py:116
  21.0 245.3 %copy-start.42 = (f32[2048]{0:T(1024)}, f32[2048]{0:T(1024)S(1)}, u32[]{:S(2)}) copy-start(f32[2048]{0:T(1024)S(1)} %convert_element_type.74) | copy-start | bytes 24580
  22.1 244.2 %copy-start.67 = (f32[1,512]{1,0:T(1,128)}, f32[1,512]{1,0:T(1,128)S(1)}, u32[]{:S(2)}) copy-start(f32[1,512]{1,0:T(1,128)S(1)} %get-tuple-element.366) | copy-start | bytes 6148
  22.1 244.2 %copy-start.69 = (f32[1,512]{1,0:T(1,128)}, f32[1,512]{1,0:T(1,128)S(1)}, u32[]{:S(2)}) copy-start(f32[1,512]{1,0:T(1,128)S(1)} %get-tuple-element.367) | copy-start | bytes 6148
  22.1 244.2 %copy-start.71 = (f32[1,512]{1,0:T(1,128)}, f32[1,512]{1,0:T(1,128)S(1)}, u32[]{:S(2)}) copy-start(f32[1,512]{1,0:T(1,128)S(1)} %get-tuple-element.364) | copy-start | bytes 6148
  22.1 244.2 %copy-start.73 = (f32[1,512]{1,0:T(1,128)}, f32[1,512]{1,0:T(1,128)S(1)}, u32[]{:S(2)}) copy-start(f32[1,512]{1,0:T(1,128)S(1)} %get-tuple-element.365) | copy-start | bytes 6148
  22.1 244.1 %copy-start.48 = (f32[2048]{0:T(1024)}, f32[2048]{0:T(1024)S(1)}, u32[]{:S(2)}) copy-start(f32[2048]{0:T(1024)S(1)} %get-tuple-element.362) | copy-start | bytes 24580
  22.2 244.1 %copy-start.50 = (f32[2048]{0:T(1024)}, f32[2048]{0:T(1024)S(1)}, u32[]{:S(2)}) copy-start(f32[2048]{0:T(1024)S(1)} %get-tuple-element.360) | copy-start | bytes 24580
  22.2 244.1 %copy-start.52 = (f32[2048]{0:T(1024)}, f32[2048]{0:T(1024)S(1)}, u32[]{:S(2)}) copy-start(f32[2048]{0:T(1024)S(1)} %get-tuple-element.361) | copy-start | bytes 24580
  22.2 244.1 %copy-start.54 = (f32[2048]{0:T(1024)}, f32[2048]{0:T(1024)S(1)}, u32[]{:S(2)}) copy-start(f32[2048]{0:T(1024)S(1)} %get-tuple-element.363) | copy-start | bytes 24580
  22.2 350.4 %copy-start.45 = (f32[2048]{0:T(1024)}, f32[2048]{0:T(1024)S(1)}, u32[]{:S(2)}) copy-start(f32[2048]{0:T(1024)S(1)} %get-tuple-element.359) | copy-start | bytes 24580
  156.3 110.1 %copy-start.77 = (f32[512]{0:T(512)S(1)}, f32[512]{0:T(512)}, u32[]{:S(2)}) copy-start(f32[512]{0:T(512)} %param.24) | copy-start | bytes 6148
  288.1 76.9 %copy-start.30 = (bf16[128,512]{1,0:T(8,128)(2,1)S(1)}, bf16[128,512]{1,0:T(8,128)(2,1)}, u32[]{:S(2)}) copy-start(bf16[128,512]{1,0:T(8,128)(2,1)} %param.28) | copy-start | bytes 393220
  288.1 76.9 %copy-start.64 = (f32[512]{0:T(512)S(1)}, f32[512]{0:T(512)}, u32[]{:S(2)}) copy-start(f32[512]{0:T(512)} %param.29) | copy-start | bytes 6148
  364.5 1236.3 %all-reduce.48.cloned.1.call-start = ((), (), s32[]{:S(2)}) async-start(), calls=%async_computation.6 | async-start | bytes 8388608 | tf_op jit(solution)/shard_map/psum | solution.py:169
  1515.1 85.7 %copy-start.65 = (f32[512]{0:T(512)S(1)}, f32[512]{0:T(512)}, u32[]{:S(2)}) copy-start(f32[512]{0:T(512)} %param.29) | copy-start | bytes 6148
  1515.1 323.8 %all-reduce.50.cloned.1.call-start = ((), (), s32[]{:S(2)}) async-start(), calls=%async_computation.8 | async-start | bytes 16777216 | tf_op jit(solution)/shard_map/psum | solution.py:127
  1606.0 75.1 %copy-start.61 = (bf16[512,4]{0,1:T(4,128)(2,1)S(1)}, bf16[512,4]{0,1:T(4,128)(2,1)}, u32[]{:S(2)}) copy-start(bf16[512,4]{0,1:T(4,128)(2,1)} %param.26) | copy-start | bytes 12292
  1687.4 151.5 %copy-start.22 = (bf16[2048,128]{1,0:T(8,128)(2,1)S(1)}, bf16[2048,128]{1,0:T(8,128)(2,1)}, u32[]{:S(2)}) copy-start(bf16[2048,128]{1,0:T(8,128)(2,1)} %get-tuple-element.280) | copy-start | bytes 1572868
  1687.4 151.5 %copy-start.33 = (bf16[512,128]{1,0:T(8,128)(2,1)S(1)}, bf16[512,128]{1,0:T(8,128)(2,1)}, u32[]{:S(2)}) copy-start(bf16[512,128]{1,0:T(8,128)(2,1)} %param.25) | copy-start | bytes 393220
  1687.4 151.5 %copy-start.43 = (f32[2048]{0:T(1024)S(1)}, f32[2048]{0:T(1024)}, u32[]{:S(2)}) copy-start(f32[2048]{0:T(1024)} %copy-done.42) | copy-start | bytes 24580
  1687.4 151.5 %copy-start.51 = (f32[2048]{0:T(1024)S(1)}, f32[2048]{0:T(1024)}, u32[]{:S(2)}) copy-start(f32[2048]{0:T(1024)} %copy-done.50) | copy-start | bytes 24580
  1687.4 151.5 %copy-start.53 = (f32[2048]{0:T(1024)S(1)}, f32[2048]{0:T(1024)}, u32[]{:S(2)}) copy-start(f32[2048]{0:T(1024)} %copy-done.52) | copy-start | bytes 24580
  1687.4 151.5 %copy-start.55 = (f32[2048]{0:T(1024)S(1)}, f32[2048]{0:T(1024)}, u32[]{:S(2)}) copy-start(f32[2048]{0:T(1024)} %copy-done.54) | copy-start | bytes 24580
  1687.4 151.5 %copy-start.66 = (f32[512]{0:T(512)S(1)}, f32[512]{0:T(512)}, u32[]{:S(2)}) copy-start(f32[512]{0:T(512)} %param.31) | copy-start | bytes 6148
  1687.5 482.1 %reduce-scatter.5.cloned.1.call-start = ((), (), s32[]{:S(2)}) async-start(), calls=%async_computation.7 | async-start | bytes 18874368 | tf_op jit(solution)/shard_map/reduce_scatter | solution.py:203
  1886.4 569.0 %reduce-scatter.3.cloned.1.call-start = ((), (), s32[]{:S(2)}) async-start(), calls=%async_computation.4 | async-start | bytes 18874368 | tf_op jit(solution)/shard_map/reduce_scatter | solution.py:132
  1932.9 236.7 %copy-start.44 = (f32[2048]{0:T(1024)S(1)}, f32[2048]{0:T(1024)}, u32[]{:S(2)}) copy-start(f32[2048]{0:T(1024)} %param.21) | copy-start | bytes 24580
  1932.9 236.7 %copy-start.63 = (f32[256]{0:T(256)S(1)}, f32[256]{0:T(256)}, u32[]{:S(2)}) copy-start(f32[256]{0:T(256)} %copy-done.62) | copy-start | bytes 3076
  (56 other events, 691.8 us)
Sparse Core Ops, SparseCore 0:
  12.7 127.6 all-gather.2
  143.1 123.1 all-gather.4
  364.6 68.4 all-reduce.45
  1515.2 85.5 all-reduce.47
  1687.6 151.2 all-reduce.49
  1886.5 282.9 reduce-scatter.4
  2173.3 282.0 reduce-scatter.2
where the time goes:
time: 2520 us; the launch traced here: 2470 us
  waiting for transfers between devices  951 us (38%)
  local copies, waits for them, and re-layouts  842 us (33%)
  other arithmetic  370 us (15%)
  blocking collectives  164 us (7%)
  matrix products  126 us (5%)
    reduce_scatter x1, waiting for transfers between devices, shards(): lax.psum_scatter(jnp.dot(gated_rows, out_weight, preferred_element_type=j...  262 us
    reduce_scatter x1, waiting for transfers between devices, shards(): lax.psum_scatter(lax.dot_general(chosen, in_flat, contract_cols, preferre...  226 us
    dynamic_update_slice x32, other arithmetic, linear_scan(): lax.scan(advance, initial, (factors, sources))  152 us
    psum x1, waiting for transfers between devices, shards(): scanned = lax.psum(scan_part, 'state')  151 us
    dynamic_slice x16, local copies, waits for them, and re-layouts, linear_scan(): lax.scan(advance, initial, (factors, sources))  142 us
    rev x1, local copies, waits for them, and re-layouts, shards(): jnp.flip(emitted, 0)  128 us
    rev x1, local copies, waits for them, and re-layouts, shards(): jnp.flip(following, 0)  128 us
    rev x1, local copies, waits for them, and re-layouts, shards(): jnp.flip(linear_scan(jnp.flip(following, 0), jnp.flip(emitted, 0)), 0)  128 us
  transfers between devices with their start and end apart: 7, of which 6 were waited for; matrix products, arithmetic and copies ran while one was open for 10% of the time, Pallas kernels for 0%

commit v1 on v0

v1 whole, which is shorter than its diff:
```python
import functools
import math

import jax
import jax.numpy as jnp
from jax import lax
from jax.experimental import pallas as pl
from jax.experimental.pallas import tpu as pltpu
from jax.sharding import PartitionSpec as P

epsilon = 1e-05
GROUP = 16
CHUNK = 256
HALO = 4
FAR = 1e30
wide = jnp.float32
low = jnp.bfloat16


def positions(lengths, tokens_all):
    ends = jnp.cumsum(lengths)
    begins = ends - lengths
    places = jnp.arange(tokens_all, dtype=jnp.int32)
    opening = jnp.max(jnp.where(begins[:, None] <= places[None, :], begins[:, None], 0), axis=0)
    return places - opening


def silu_slope(values):
    logistic = jax.nn.sigmoid(values)
    return logistic * (1.0 + values * (1.0 - logistic))


def own_block(states):
    row = lax.broadcasted_iota(jnp.int32, (GROUP, GROUP * states), 0)
    col = lax.broadcasted_iota(jnp.int32, (GROUP, GROUP * states), 1)
    return jnp.logical_and(col >= row * states, col < (row + 1) * states)


def forward_body(step_ref, drive_ref, coeff_ref, entry_ref, read_ref, y_ref, state_ref, carry):
    @pl.when(pl.program_id(0) == 0)
    def _():
        carry[...] = jnp.zeros_like(carry)

    coeff = coeff_ref[...]
    states = coeff.shape[0]
    chosen = own_block(states)

    def group(index, state):
        base = pl.multiple_of(index * GROUP, GROUP)
        entry = entry_ref[index]
        kept = []
        for i in range(GROUP):
            decay = jnp.exp2(step_ref[pl.ds(base + i, 1), :] * coeff)
            state = decay * state + drive_ref[pl.ds(base + i, 1), :] * entry[:, i : i + 1]
            kept.append(state)
        rows = pl.multiple_of(base * states, GROUP * states)
        block = jnp.concatenate(kept, axis=0).astype(low)
        state_ref[pl.ds(rows, GROUP * states), :] = block
        weights = jnp.where(chosen, read_ref[index], 0.0).astype(low)
        y_ref[pl.ds(base, GROUP), :] = jnp.dot(weights, block, preferred_element_type=wide)
        return state

    carry[...] = lax.fori_loop(0, step_ref.shape[0] // GROUP, group, carry[...])


def backward_body(
    step_ref,
    delta_ref,
    drive_ref,
    dmix_ref,
    coeff_ref,
    entry_ref,
    read_ref,
    state_ref,
    before_ref,
    lam_ref,
    flow_ref,
    dentry_ref,
    dread_ref,
    decay_ref,
    carry,
    total,
):
    turn = pl.program_id(0)

    @pl.when(turn == 0)
    def _():
        carry[...] = jnp.zeros_like(carry)
        total[...] = jnp.zeros_like(total)

    coeff = coeff_ref[...]
    states = coeff.shape[0]
    chosen = own_block(states)
    groups = step_ref.shape[0] // GROUP
    first = jnp.where(turn == pl.num_programs(0) - 1, 0.0, before_ref[...].astype(wide))
    across = (((1,), (1,)), ((), ()))

    def group(turned, totals):
        pulled, summed = totals
        index = groups - 1 - turned
        base = pl.multiple_of(index * GROUP, GROUP)
        rows = pl.multiple_of(base * states, GROUP * states)
        read = read_ref[index]
        block = state_ref[pl.ds(rows, GROUP * states), :]
        block_wide = block.astype(wide)
        prior = pl.multiple_of(jnp.maximum(rows - states, 0), states)
        edge = jnp.where(index == 0, first, state_ref[pl.ds(prior, states), :].astype(wide))
        lams = [None] * GROUP
        flows = [None] * GROUP
        for i in range(GROUP - 1, -1, -1):
            lam = read[:, i : i + 1] * dmix_ref[pl.ds(base + i, 1), :] + pulled
            pulled = jnp.exp2(step_ref[pl.ds(base + i, 1), :] * coeff) * lam
            earlier = block_wide[(i - 1) * states : i * states] if i else edge
            flow = pulled * earlier
            summed = summed + flow * delta_ref[pl.ds(base + i, 1), :]
            lams[i] = lam
            flows[i] = flow * coeff
        lam_block = jnp.concatenate(lams, axis=0).astype(low)
        flow_block = jnp.concatenate(flows, axis=0).astype(low)
        here = pl.ds(base, GROUP)
        weights = jnp.where(chosen, entry_ref[index], 0.0).astype(low)
        lam_ref[here, :] = jnp.dot(weights, lam_block, preferred_element_type=wide)
        ones = jnp.where(chosen, 1.0, 0.0).astype(low)
        flow_ref[here, :] = jnp.dot(ones, flow_block, preferred_element_type=wide)
        cross = lax.dot_general(
            drive_ref[here, :].astype(low), lam_block, across, preferred_element_type=wide
        )
        dentry_ref[index] = jnp.sum(jnp.where(chosen, cross, 0.0), axis=0, keepdims=True)
        cross = lax.dot_general(
            dmix_ref[here, :].astype(low), block, across, preferred_element_type=wide
        )
        dread_ref[index] = jnp.sum(jnp.where(chosen, cross, 0.0), axis=0, keepdims=True)
        return pulled, summed

    pulled, summed = lax.fori_loop(0, groups, group, (carry[...], total[...]))
    carry[...] = pulled
    total[...] = summed
    decay_ref[...] = summed


def per_group(values):
    tokens, states = values.shape
    return jnp.swapaxes(values.reshape(tokens // GROUP, GROUP, states), 1, 2)


def forward_scan(step, drive, coeff, entry, readout):
    tokens, width = step.shape
    states = coeff.shape[0]
    many = CHUNK // GROUP
    row = pl.BlockSpec((CHUNK, width), lambda t: (t, 0))
    return pl.pallas_call(
        forward_body,
        grid=(tokens // CHUNK,),
        in_specs=[
            row,
            row,
            pl.BlockSpec((states, width), lambda t: (0, 0)),
            pl.BlockSpec((many, states, GROUP), lambda t: (t, 0, 0)),
            pl.BlockSpec((many, 1, GROUP * states), lambda t: (t, 0, 0)),
        ],
        out_specs=[row, pl.BlockSpec((CHUNK * states, width), lambda t: (t, 0))],
        out_shape=[
            jax.ShapeDtypeStruct((tokens, width), wide),
            jax.ShapeDtypeStruct((tokens * states, width), low),
        ],
        scratch_shapes=[pltpu.VMEM((states, width), wide)],
        compiler_params=pltpu.CompilerParams(vmem_limit_bytes=24 * 1024 * 1024),
        name="forward_scan",
    )(step, drive, coeff, per_group(entry), readout.reshape(tokens // GROUP, 1, GROUP * states))


def backward_scan(step, delta, drive, dmix, coeff, entry, readout, kept):
    tokens, width = step.shape
    states = coeff.shape[0]
    many = CHUNK // GROUP
    last = tokens // CHUNK - 1
    row = pl.BlockSpec((CHUNK, width), lambda t: (last - t, 0))
    flat = pl.BlockSpec((many, 1, GROUP * states), lambda t: (last - t, 0, 0))
    fixed = pl.BlockSpec((states, width), lambda t: (0, 0))
    return pl.pallas_call(
        backward_body,
        grid=(tokens // CHUNK,),
        in_specs=[
            row,
            row,
            row,
            row,
            fixed,
            flat,
            pl.BlockSpec((many, states, GROUP), lambda t: (last - t, 0, 0)),
            pl.BlockSpec((CHUNK * states, width), lambda t: (last - t, 0)),
            pl.BlockSpec(
                (states, width), lambda t: (jnp.maximum((last - t) * CHUNK - 1, 0), 0)
            ),
        ],
        out_specs=[row, row, flat, flat, fixed],
        out_shape=[
            jax.ShapeDtypeStruct((tokens, width), wide),
            jax.ShapeDtypeStruct((tokens, width), wide),
            jax.ShapeDtypeStruct((tokens // GROUP, 1, GROUP * states), wide),
            jax.ShapeDtypeStruct((tokens // GROUP, 1, GROUP * states), wide),
            jax.ShapeDtypeStruct((states, width), wide),
        ],
        scratch_shapes=[pltpu.VMEM((states, width), wide), pltpu.VMEM((states, width), wide)],
        compiler_params=pltpu.CompilerParams(vmem_limit_bytes=24 * 1024 * 1024),
        name="backward_scan",
    )(
        step,
        delta,
        drive,
        dmix,
        coeff,
        entry.reshape(tokens // GROUP, 1, GROUP * states),
        per_group(readout),
        kept,
        kept,
    )


def shards(
    n_chan,
    n_state,
    hidden_in,
    norm_gain,
    in_weight,
    conv_kernel,
    conv_offset,
    select_rank,
    select_entry,
    select_read,
    delta_weight,
    step_bias,
    decay_log,
    skip_weight,
    out_weight,
    lengths,
    pad_mask,
    cotangent,
):
    rows_dev, width = hidden_in.shape
    tokens = pad_mask.shape[0]
    chans = in_weight.shape[2]
    taps = conv_kernel.shape[0]
    rank = select_rank.shape[1]
    per_state = select_entry.shape[1]
    states = per_state * n_state
    small = rank + 2 * states
    quarter = rows_dev // n_state
    own = chans // n_state
    part = lax.axis_index("state")
    contract_rows = (((0,), (0,)), ((), ()))
    contract_cols = (((1,), (1,)), ((), ()))

    def gather_chan(values):
        return lax.all_gather(values, "chan", axis=0)

    def gather_state(values):
        return lax.all_gather(values, "state", axis=0)

    def swap_state(values):
        return lax.all_to_all(values, "state", 0, 0, tiled=True)

    def sum_chan(parts):
        moved = lax.all_to_all(parts, "chan", 0, 0, tiled=True)
        return jnp.sum(moved.astype(wide), axis=0)

    def mine(values, axis=0):
        return lax.dynamic_slice_in_dim(values, part * own, own, axis)

    def windows(values, before, after):
        tail = values.shape[1:]
        groups = values.reshape((n_chan * n_state, quarter) + tail)
        pieces = [groups]
        if before:
            pad = jnp.zeros((1, before) + tail, values.dtype)
            pieces.insert(0, jnp.concatenate([pad, groups[:-1, quarter - before :]], axis=0))
        if after:
            pad = jnp.zeros((1, after) + tail, values.dtype)
            pieces.append(jnp.concatenate([groups[1:, :after], pad], axis=0))
        joined = jnp.concatenate(pieces, axis=1)
        return joined.reshape((n_chan, n_state) + joined.shape[1:])

    def window_of(values, before, after):
        found = windows(values, before, after)
        return lax.dynamic_index_in_dim(found, part, axis=1, keepdims=False)

    def to_tokens(values):
        return jnp.swapaxes(values, 0, 1).reshape((tokens,) + values.shape[3:])

    def split_own(values):
        lead = values.shape[:-1]
        cut = values.reshape(lead + (n_state, own))
        return jnp.moveaxis(cut, -2, 0)

    def join_own(values):
        moved = jnp.moveaxis(values, 0, -2)
        return moved.reshape(moved.shape[:-2] + (chans,))

    place = positions(lengths, tokens)
    maskf = pad_mask.astype(wide)
    place_win = window_of(place, HALO, HALO)
    mask_win = window_of(maskf, HALO, HALO)[:, :, None]

    start = part * quarter
    hidden_q = lax.dynamic_slice_in_dim(hidden_in, start, quarter, 0)
    ahead = lax.rem(start + rows_dev - HALO, rows_dev)
    behind = lax.rem(start + quarter, rows_dev)
    local = jnp.concatenate(
        [
            hidden_q,
            lax.dynamic_slice_in_dim(hidden_in, ahead, HALO, 0),
            lax.dynamic_slice_in_dim(hidden_in, behind, HALO, 0),
        ],
        axis=0,
    )
    inv_all = lax.rsqrt(jnp.mean(local * local, axis=1, keepdims=True) + epsilon)
    scaled_all = local * inv_all
    normed_all = (scaled_all * norm_gain[None, :]).astype(low)
    inv_rms = inv_all[:quarter]
    scaled = scaled_all[:quarter]
    gathered = gather_chan(normed_all)
    normed_q = gathered[:, :quarter].reshape(n_chan * quarter, width)

    cot_q = lax.dynamic_slice_in_dim(cotangent, start, quarter, 0)
    grad_q = gather_chan(cot_q.astype(low)).reshape(n_chan * quarter, width)

    columns = jnp.concatenate([select_entry, select_read], axis=1)
    columns = gather_state(columns).reshape(n_state, chans, 2, per_state)
    columns = jnp.transpose(columns, (1, 2, 0, 3)).reshape(chans, 2 * states)
    select = jnp.concatenate([select_rank, columns], axis=1)
    decay_own = swap_state(jnp.swapaxes(decay_log.reshape(per_state, n_state, own), 0, 1))
    coeff = -jnp.exp(decay_own.reshape(states, own))

    in_flat = in_weight.reshape(width, 2 * chans)
    both = jnp.dot(
        gathered.reshape(-1, width), in_flat, preferred_element_type=wide
    ).reshape(n_chan, quarter + 2 * HALO, 2 * chans)
    gate_q = both[:, :quarter, chans:].astype(low)
    raw = both[:, :, :chans].astype(low)
    nothing = jnp.zeros((1, HALO, chans), low)
    before = raw[:, quarter : quarter + HALO]
    before = jnp.where(part == 0, jnp.concatenate([nothing, before[:-1]], axis=0), before)
    after = raw[:, quarter + HALO :]
    after = jnp.where(
        part == n_state - 1, jnp.concatenate([after[1:], nothing], axis=0), after
    )
    inner_win = jnp.concatenate([before, raw[:, :quarter], after], axis=1) * mask_win

    def convolve(values, places, span):
        total = conv_offset
        for index in range(taps):
            lag = taps - 1 - index
            valid = (places >= lag).astype(wide)[..., None]
            first = taps - 1 - lag
            total = total + conv_kernel[index] * values[:, first : first + span] * valid
        return total

    span = quarter + HALO
    conv_win = convolve(inner_win[:, HALO - taps + 1 :], place_win[:, HALO:], span)
    act_q = (jax.nn.silu(conv_win[:, :quarter]) * mask_win[:, HALO : HALO + quarter]).astype(low)
    act_q = act_q.reshape(n_chan * quarter, chans)

    partial = jnp.dot(act_q, select, preferred_element_type=wide)
    summed = sum_chan(partial.reshape(n_chan, quarter, small))
    picked = lax.all_gather(summed.astype(low), ("chan", "state"), axis=0, tiled=True)
    lowrank = picked[:, :rank]
    entry = picked[:, rank : rank + states].astype(wide)
    readout = picked[:, rank + states :].astype(wide)

    sent = jnp.stack([raw[:, :quarter], gate_q], axis=2)
    moved = to_tokens(swap_state(split_own(sent)))
    inner_own = moved[:, 0].astype(wide) * maskf[:, None]
    gate_own = moved[:, 1].astype(wide)
    kernel_own = mine(conv_kernel, 1)
    offset_own = mine(conv_offset)
    conv_own = offset_own[None, :]
    for index in range(taps):
        lag = taps - 1 - index
        valid = (place >= lag).astype(wide)[:, None]
        shifted = jnp.pad(inner_own, ((lag, 0), (0, 0)))[:tokens]
        conv_own = conv_own + kernel_own[index][None, :] * shifted * valid
    act_own = (jax.nn.silu(conv_own) * maskf[:, None]).astype(low)
    act_wide = act_own.astype(wide)
    weight_own = mine(delta_weight, 1)
    dpre = jnp.dot(lowrank, weight_own, preferred_element_type=wide) + mine(step_bias)[None, :]
    delta = jax.nn.softplus(dpre)
    drive = delta * act_wide
    step = jnp.where((place > 0)[:, None], delta, FAR)
    coeff_two = coeff * math.log2(math.e)
    scanned, kept = forward_scan(step, drive, coeff_two, entry, readout)
    skip_own = mine(skip_weight)
    mixed = scanned + skip_own[None, :] * act_wide
    gate_act = jax.nn.silu(gate_own)
    gated = (mixed * gate_act).astype(low)

    dgated_q = lax.dot_general(grad_q, out_weight, contract_cols, preferred_element_type=wide)
    dgated_q = dgated_q.astype(low).reshape(n_chan, quarter, chans)
    dgated = to_tokens(swap_state(split_own(dgated_q))).astype(wide)
    dmix = dgated * gate_act
    dgate = (dgated * mixed * silu_slope(gate_own)).astype(low)
    skip_grad_own = jnp.sum(dmix * act_wide, axis=0)

    lam_sum, flow_sum, dentry, dread, flow_total = backward_scan(
        step, delta, drive, dmix, coeff_two, entry, readout, kept
    )
    scale = 1.0 / math.log2(math.e)
    decay_grad_own = coeff * flow_total
    ddelta = flow_sum * scale + lam_sum * act_wide
    ddpre = (ddelta * jax.nn.sigmoid(dpre)).astype(low)
    bias_grad_own = jnp.sum(ddpre.astype(wide), axis=0)
    delta_grad_own = lax.dot_general(lowrank, ddpre, contract_rows, preferred_element_type=wide)
    dlow = lax.dot_general(ddpre, weight_own, contract_cols, preferred_element_type=wide)
    partial = jnp.concatenate(
        [dlow, dentry.reshape(tokens, states), dread.reshape(tokens, states)], axis=1
    )
    parts = windows(partial.astype(low), 0, HALO)
    parts = lax.all_to_all(
        parts.reshape((n_chan * n_state,) + parts.shape[2:]),
        ("chan", "state"),
        0,
        0,
        tiled=True,
    )
    dsmall = gather_chan(jnp.sum(parts.astype(wide), axis=0).astype(low))

    gated_all = gather_state(jnp.moveaxis(gated.reshape(n_chan, n_state, quarter, own), 1, 0))
    gated_all = jnp.moveaxis(gated_all, 0, 3).reshape(n_state, n_chan * quarter, chans)
    gated_q = lax.dynamic_index_in_dim(gated_all, part, axis=0, keepdims=False)
    branch = jnp.dot(gated_q, out_weight, preferred_element_type=wide).astype(low)
    branch = sum_chan(branch.reshape(n_chan, quarter, width))
    branch = gather_state(branch.astype(low)).reshape(rows_dev, width)
    result = hidden_in + branch
    grad_all = gather_state(grad_q).reshape(tokens, width)
    out_grad = lax.dot_general(
        gated_all.reshape(tokens, chans), grad_all, contract_rows, preferred_element_type=wide
    )

    reach = quarter + HALO
    dscan = lam_sum * delta + dmix * skip_own[None, :]
    dscan = jnp.swapaxes(windows(dscan.astype(low), 0, HALO), 0, 1)
    dscan_win = join_own(swap_state(dscan)).astype(wide)
    dact = dscan_win + lax.dot_general(
        dsmall.reshape(-1, small), select, contract_cols, preferred_element_type=wide
    ).reshape(n_chan, reach, chans)
    dconv = dact * mask_win[:, HALO:] * silu_slope(conv_win)
    dinner = jnp.zeros((n_chan, quarter, chans), wide)
    kernel_rows = []
    for index in range(taps):
        lag = taps - 1 - index
        valid = (place_win[:, HALO:] >= lag).astype(wide)[..., None]
        masked = dconv * valid
        kernel_rows.append(
            jnp.sum(
                masked[:, :quarter] * inner_win[:, HALO - lag : HALO - lag + quarter], axis=(0, 1)
            )
        )
        dinner = dinner + masked[:, lag : lag + quarter] * conv_kernel[index]
    kernel_rows.append(jnp.sum(dconv[:, :quarter], axis=(0, 1)))
    dinner = (dinner * mask_win[:, HALO : HALO + quarter]).astype(low)
    dgate_q = jnp.swapaxes(dgate.reshape(n_chan, n_state, quarter, own), 0, 1)
    dgate_q = join_own(swap_state(dgate_q))
    dboth = jnp.concatenate([dinner, dgate_q], axis=2).reshape(n_chan * quarter, 2 * chans)

    dnormed = lax.dot_general(dboth, in_flat, contract_cols, preferred_element_type=wide)
    gain_part = jnp.sum(dnormed * normed_q.astype(wide), axis=0)
    dnormed = sum_chan(dnormed.astype(low).reshape(n_chan, quarter, width))
    gain_grad = lax.psum(gain_part, ("chan", "state")) / norm_gain
    dscaled = dnormed * norm_gain[None, :]
    change = inv_rms * (dscaled - scaled * jnp.mean(dscaled * scaled, axis=1, keepdims=True))
    input_grad = cotangent + gather_state(change.astype(low)).reshape(rows_dev, width)

    dboth_all = gather_state(dboth).reshape(tokens, 2 * chans)
    normed_rows = gather_state(normed_q).reshape(tokens, width)
    in_grad = lax.dot_general(
        normed_rows, dboth_all, contract_rows, preferred_element_type=wide
    ).reshape(width, 2, chans)

    dsmall_q = dsmall[:, :quarter].reshape(n_chan * quarter, small)
    select_grad = lax.dot_general(act_q, dsmall_q, contract_rows, preferred_element_type=wide)
    rest = lax.psum((select_grad, jnp.stack(kernel_rows)), "state")
    select_grad, kernel_rows = rest
    rank_grad = select_grad[:, :rank]
    first = rank + part * per_state
    entry_grad = lax.dynamic_slice_in_dim(select_grad, first, per_state, 1)
    read_grad = lax.dynamic_slice_in_dim(select_grad, first + states, per_state, 1)
    kernel_grad = kernel_rows[:taps]
    offset_grad = kernel_rows[taps]
    packed = jnp.concatenate(
        [delta_grad_own, decay_grad_own, bias_grad_own[None], skip_grad_own[None]], axis=0
    )
    packed = jnp.swapaxes(gather_state(packed), 0, 1).reshape(-1, chans)
    delta_grad = packed[:rank]
    decay_grad = lax.dynamic_slice_in_dim(packed, rank + part * per_state, per_state, 0)
    bias_grad = packed[rank + states]
    skip_grad = packed[rank + states + 1]
    return (
        result,
        input_grad,
        gain_grad,
        in_grad,
        kernel_grad,
        offset_grad,
        rank_grad,
        entry_grad,
        read_grad,
        delta_grad,
        bias_grad,
        decay_grad,
        skip_grad,
        out_grad,
    )


def solution(mesh):
    sizes = dict(mesh.shape)
    return jax.shard_map(
        functools.partial(shards, sizes["chan"], sizes["state"]),
        mesh=mesh,
        in_specs=(
            P("chan", None),
            P(),
            P(None, None, "chan"),
            P(None, "chan"),
            P("chan"),
            P("chan", None),
            P("chan", "state"),
            P("chan", "state"),
            P(None, "chan"),
            P("chan"),
            P("state", "chan"),
            P("chan"),
            P("chan", None),
            P(),
            P(),
            P("chan", None),
        ),
        out_specs=(
            P("chan", None),
            P("chan", None),
            P(),
            P(None, None, "chan"),
            P(None, "chan"),
            P("chan"),
            P("chan", None),
            P("chan", "state"),
            P("chan", "state"),
            P(None, "chan"),
            P("chan"),
            P("state", "chan"),
            P("chan"),
            P("chan", None),
        ),
        check_vma=False,
    )
```

time: 2520 us -> 689 us (0.27); the launches traced: 2470 us -> 681 us
  local copies, waits for them, and re-layouts: 842 us -> 86.6 us
  waiting for transfers between devices: 951 us -> 200 us
  other arithmetic: 370 us -> 38.1 us
  matrix products: 126 us -> 46.9 us
  Pallas kernels: 0 us -> 69.7 us
  starting transfers between devices: 0.75 us -> 31.9 us
  blocking collectives: 164 us -> 192 us
    reduce_scatter x2 -> x0, waiting for transfers between devices: 488 us -> none  [the longest x1 262 us: shards(): lax.psum_scatter(jnp.dot(gated_rows, out_weight, preferred_element_type=j...]
    rev x3 -> x0, local copies, waits for them, and re-layouts: 383 us -> none  [the longest x1 128 us: shards(): jnp.flip(emitted, 0)]
    psum x3 -> x1, waiting for transfers between devices: 237 us -> 0.01 us  [shards(): rest = lax.psum((select_grad, jnp.stack(kernel_rows)), 'state')]
    dynamic_update_slice x32 -> x0, other arithmetic: 152 us -> none  [linear_scan(): lax.scan(advance, initial, (factors, sources))]
    dynamic_slice x16 -> x8, local copies, waits for them, and re-layouts: 142 us -> 6.01 us  [the longest x4 2.08 us: mine(): return lax.dynamic_slice_in_dim(values, part * own, own, axis)]
    psum x3 -> x2, blocking collectives: 164 us -> 51.3 us  [the longest x1 39.4 us: shards(): gain_grad = lax.psum(gain_part, ('chan', 'state')) / norm_gain]
    pad x20 -> x0, local copies, waits for them, and re-layouts: 110 us -> none  [linear_scan(): lax.associative_scan(combine, (products[-1], local_states[-1]), axis=0)]
    all_gather x2 -> x8, waiting for transfers between devices: 226 us -> 125 us  [the longest x2 73.5 us: gather_chan(): return lax.all_gather(values, 'chan', axis=0)]
  transfers between devices with their start and end apart: 7 -> 17, of which waited for: 6 -> 9; matrix products, arithmetic and copies ran while one was open for 10% -> 17% of each run, Pallas kernels for 0% -> 0%
where the time goes in v1:
time: 689 us; the launch traced here: 681 us
  waiting for transfers between devices  200 us (29%)
  blocking collectives  192 us (28%)
  local copies, waits for them, and re-layouts  86.6 us (13%)
  Pallas kernels  69.7 us (10%)
  matrix products  46.9 us (7%)
  other arithmetic  38.1 us (6%)
  starting transfers between devices  31.9 us (5%)
  between operations  15.5 us (2%)
    all_gather x2, waiting for transfers between devices, gather_chan(): return lax.all_gather(values, 'chan', axis=0)  73.5 us
    all_gather x6, waiting for transfers between devices, gather_state(): return lax.all_gather(values, 'state', axis=0)  51.3 us
    all_to_all x1, blocking collectives, sum_chan(): moved = lax.all_to_all(parts, 'chan', 0, 0, tiled=True)  49.4 us
    all_to_all x2, waiting for transfers between devices, sum_chan(): moved = lax.all_to_all(parts, 'chan', 0, 0, tiled=True)  48.5 us
    all_gather x1, blocking collectives, shards(): lax.all_gather(summed.astype(low), ('chan', 'state'), axis=0, tiled=True)  47.6 us
    psum x1, blocking collectives, shards(): gain_grad = lax.psum(gain_part, ('chan', 'state')) / norm_gain  39.4 us
    pallas_call x1, Pallas kernels, backward_scan(): pl.pallas_call(backward_body, grid=(tokens // CHUNK,), in_specs=[row, row...  39.2 us
    all_gather x1, blocking collectives, gather_chan(): return lax.all_gather(values, 'chan', axis=0)  31.1 us
  transfers between devices with their start and end apart: 17, of which 9 were waited for; matrix products, arithmetic and copies ran while one was open for 17% of the time, Pallas kernels for 0%

profile of v1, /device:TPU:0, one launch (start us, length us, event | category | flops | bytes accessed | tf_op | source)
XLA Modules:
  0.0 680.9 jit_solution(14387268985699364622)
XLA Ops:
  14.3 4.2 all-to-all-start.2
  19.8 5.3 all-gather
  25.2 7.7 %reshape.416 = bf16[2048,1024,1]{1,0,2:T(8,128)(2,1)} reshape(bf16[2048,2,512]{2,1,0:T(2,128)(2,1)} %param.18) | data formatting | bytes 8388608 | tf_op jit(solution)/shard_map/reshape | solution.py:334
  35.2 27.6 %all-gather.29.cloned.1.call-done = bf16[512,2048]{1,0:T(8,128)(2,1)} async-done(((bf16[64,2048]{1,0:T(8,128)(2,1)}), bf16[512,2048]{1,0:T(8,128)(2,1)}) %all-gather.29.cloned.1.call-update) | async-done | bytes 2097168 | tf_op jit(solution)/shard_map/all_gather | solution.py:255
  70.2 46.0 %all-gather.19.cloned.1.call-done = bf16[8,72,2048]{2,1,0:T(8,128)(2,1)} async-done(((bf16[1,72,2048]{2,1,0:T(8,128)(2,1)}), bf16[8,72,2048]{2,1,0:T(8,128)(2,1)}) %all-gather.19.cloned.1.call-update) | async-done | bytes 2359312 | tf_op jit(solution)/shard_map/all_gather | solution.py:255
  116.1 5.5 convolution_convert_fusion.2
  126.9 4.1 all-to-all-start
  135.7 8.9 %all-to-all-done = f32[8,64,160]{2,1,0:T(8,128)} async-done(((f32[8,64,160]{2,1,0:T(8,128)}), f32[8,64,160]{2,1,0:T(8,128)}, u32[]{:S(2)}, u32[]{:S(2)}) %all-to-all-start) | async-done | bytes 327712 | tf_op jit(solution)/shard_map/all_to_all | solution.py:264
  144.6 4.3 all-to-all-start.1
  150.0 47.6 %all_gather.61 = bf16[2048,160]{1,0:T(8,128)(2,1)S(1)} all-gather(bf16[64,160]{1,0:T(8,128)(2,1)S(1)} %reduce_sum.133), channel_id=1, replica_groups=mesh['chan'=8,'state'=4] {'chan','state'}, dimensions={0}, use_global_device_ids=true | all-gather | bytes 675840 | tf_op jit(solution)/shard_map/all_gather | solution.py:365
  211.6 30.5 %forward_scan.1 = (f32[2048,128]{1,0:T(8,128)S(1)}, bf16[32768,128]{1,0:T(8,128)(2,1)S(1)}) custom-call(f32[2048,128]{1,0:T(8,128)S(1)} %get-tuple-element.142.step_ref, f32[2048,128]{1,0:T(8,128)S(1)} %get-tuple-element.143.drive_ref, f32[16,128]{1,0:T(8,128)S(1)} %broadcast_multiply_fusion.3.coeff_ref, f32[128,16,16]{2,1,0:T(8,128)S(1)} %bitcast.176, ...), custom_call_target="tpu_custom_call" | custom-call | tf_op jit(solution)/shard_map/forward_scan/pallas_call | solution.py:151
  242.1 39.2 %backward_scan.1 = (f32[2048,128]{1,0:T(8,128)S(1)}, f32[2048,128]{1,0:T(8,128)S(1)}, f32[128,1,256]{2,1,0:T(1,128)S(1)}, f32[128,1,256]{2,1,0:T(1,128)S(1)}, f32[16,128]{1,0:T(8,128)S(1)}) custom-call(f32[2048,128]{1,0:T(8,128)S(1)} %get-tuple-element.142.step_ref, f32[2048,128]{1,0:T(8,128)S(1)} %get-tuple-element.141.delta_ref, ...), custom_call_target="tpu_custom_call" | custom-call | tf_op jit(solution)/shard_map/backward_scan/pallas_call | solution.py:180
  285.2 4.1 all-to-all-start.7
  298.3 4.1 all-to-all-start.5
  305.9 5.8 all-to-all-done.5
  314.4 5.5 copy.242
  326.8 16.6 %all-to-all-done.6 = bf16[32,68,160]{2,1,0:T(8,128)(2,1)S(1)} async-done(((bf16[32,68,160]{2,1,0:T(8,128)(2,1)}), bf16[32,68,160]{2,1,0:T(8,128)(2,1)S(1)}, u32[]{:S(2)}, u32[]{:S(2)}) %all-to-all-start.6) | async-done | bytes 696352 | tf_op jit(solution)/shard_map/all_to_all | solution.py:417
  343.6 31.1 %all-gather.8 = bf16[8,68,160]{2,1,0:T(8,128)(2,1)S(1)} all-gather(bf16[1,68,160]{2,1,0:T(8,128)(2,1)S(1)} %bitcast.211), channel_id=6, replica_groups=mesh['chan'=8,'state'=4] {'chan'}, dimensions={0}, use_global_device_ids=true | all-gather | bytes 195840 | tf_op jit(solution)/shard_map/all_gather | solution.py:255
  380.8 3.7 fusion
  384.6 4.5 all-to-all-start.8
  391.2 39.6 %all-to-all-done.8 = bf16[8,64,2048]{2,1,0:T(8,128)(2,1)} async-done(((bf16[8,64,2048]{2,1,0:T(8,128)(2,1)}), bf16[8,64,2048]{2,1,0:T(8,128)(2,1)}, u32[]{:S(2)}, u32[]{:S(2)}) %all-to-all-start.8) | async-done | bytes 2097184 | tf_op jit(solution)/shard_map/all_to_all | solution.py:264
  436.5 4.9 copy.208
  441.4 4.1 reshape.375
  447.8 49.4 %all_to_all.45 = bf16[8,64,2048]{2,1,0:T(8,128)(2,1)} all-to-all(bf16[8,64,2048]{2,1,0:T(8,128)(2,1)S(1)} %bitcast.200), channel_id=1, replica_groups=mesh['chan'=8,'state'=4] {'chan'}, dimensions={0} | all-to-all | bytes 4194304 | tf_op jit(solution)/shard_map/all_to_all | solution.py:264
  502.9 7.4 %all-gather.9 = f32[4,146,128]{2,1,0:T(8,128)S(1)} all-gather(f32[1,146,128]{2,1,0:T(8,128)S(1)} %maximum_bitcast_fusion.5), channel_id=8, replica_groups=mesh['chan'=8,'state'=4] {'state'}, dimensions={0}, use_global_device_ids=true | all-gather | bytes 373760 | tf_op jit(solution)/shard_map/all_gather | solution.py:258
  513.1 11.8 %psum.22 = f32[5,512]{1,0:T(8,128)S(1)} all-reduce(f32[5,512]{1,0:T(8,128)S(1)} %stack.35), channel_id=1, replica_groups=mesh['chan'=8,'state'=4] {'state'}, use_global_device_ids=true, to_apply=%region_15.16 | all-reduce | flops 2560 | bytes 20480 | tf_op jit(solution)/shard_map/psum | solution.py:480
  526.2 39.4 %psum.21 = f32[2048]{0:T(1024)S(1)} all-reduce(f32[2048]{0:T(1024)S(1)} %get-tuple-element.125), channel_id=1, replica_groups=mesh['chan'=8,'state'=4] {'chan','state'}, use_global_device_ids=true, to_apply=%region_9.10 | all-reduce | flops 2048 | bytes 16384 | tf_op jit(solution)/shard_map/psum | solution.py:467
  572.9 6.4 copy.223
  585.0 10.7 %fusion.1 = f32[512,2048]{1,0:T(8,128)} fusion(bf16[2048,2048]{1,0:T(8,128)(2,1)} %all-gather.33.cloned.1.call-done, bf16[256,8,4,128]{3,2,1,0:T(4,128)(2,1)} %bitcast.181), kind=kOutput, calls=%fused_computation.7 | convolution fusion | flops 4294967296 | bytes 14680064 | tf_op jit(solution)/shard_map/dot_general | solution.py:434
  595.7 49.2 %all-gather.21.cloned.1.call-done = bf16[4,512,2048]{2,1,0:T(8,128)(2,1)} async-done(((bf16[1,512,2048]{2,1,0:T(8,128)(2,1)}), bf16[4,512,2048]{2,1,0:T(8,128)(2,1)}) %all-gather.21.cloned.1.call-update) | async-done | bytes 8388624 | tf_op jit(solution)/shard_map/all_gather | solution.py:258
  644.9 12.6 %fusion.82 = f32[2048,2,512]{2,0,1:T(8,128)S(1)} fusion(bf16[2048,2048,1]{1,0,2:T(8,128)(2,1)} %bitcast.246, bf16[2,512,2048]{2,1,0:T(8,128)(2,1)} %bitcast.190), kind=kOutput, calls=%fused_computation.198 | convolution fusion | flops 8589934592 | bytes 20971520 | tf_op jit(solution)/shard_map/dot_general | solution.py:474
  657.5 16.5 %copy.227 = f32[2048,2,512]{2,1,0:T(2,128)} copy(f32[2048,2,512]{2,0,1:T(8,128)S(1)} %fusion.82) | data formatting | bytes 16777216
  (270 shorter events, 107.0 us)
Async XLA Ops:
  7.2 55.6 %copy-start = (bf16[512,2048]{1,0:T(8,128)(2,1)S(1)}, bf16[512,2048]{1,0:T(8,128)(2,1)}, u32[]{:S(2)}) copy-start(bf16[512,2048]{1,0:T(8,128)(2,1)} %param.28) | copy-start | bytes 6291460
  7.2 55.6 %all-gather.29.cloned.1.call-start = ((), (), s32[]{:S(2)}) async-start(), calls=%async_computation.15 | async-start | bytes 2359296 | tf_op jit(solution)/shard_map/all_gather | solution.py:255
  9.2 106.9 %all-gather.19.cloned.1.call-start = ((), (), s32[]{:S(2)}) async-start(), calls=%async_computation.9 | async-start | bytes 2654208 | tf_op jit(solution)/shard_map/all_gather | solution.py:255
  14.3 20.9 %all-to-all-start.2 = ((f32[4,4,128]{2,1,0:T(4,128)}), f32[4,4,128]{2,1,0:T(4,128)S(1)}, u32[]{:S(2)}, u32[]{:S(2)}) async-start(f32[4,4,128]{2,1,0:T(4,128)} %bitcast.28), calls=%async_computation.2 | async-start | bytes 16384 | tf_op jit(solution)/shard_map/all_to_all | solution.py:261
  19.4 103.2 %copy-start.31 = (f32[8,1,72]{2,1,0:T(1,128)}, f32[8,1,72]{2,1,0:T(1,128)S(1)}, u32[]{:S(2)}) copy-start(f32[8,1,72]{2,1,0:T(1,128)S(1)} %fusion.69) | copy-start | bytes 6916
  19.7 104.2 %copy-start.33 = (f32[8,64]{1,0:T(8,128)}, f32[8,64]{1,0:T(8,128)S(1)}, u32[]{:S(2)}) copy-start(f32[8,64]{1,0:T(8,128)S(1)} %slice_bitcast_fusion.3) | copy-start | bytes 6148
  19.7 103.3 %copy-start.37 = (f32[1,512]{1,0:T(1,128)}, f32[1,512]{1,0:T(1,128)S(1)}, u32[]{:S(2)}) copy-start(f32[1,512]{1,0:T(1,128)S(1)} %get-tuple-element.161) | copy-start | bytes 6148
  19.7 103.3 %copy-start.39 = (f32[1,512]{1,0:T(1,128)}, f32[1,512]{1,0:T(1,128)S(1)}, u32[]{:S(2)}) copy-start(f32[1,512]{1,0:T(1,128)S(1)} %get-tuple-element.162) | copy-start | bytes 6148
  19.7 103.3 %copy-start.41 = (f32[1,512]{1,0:T(1,128)}, f32[1,512]{1,0:T(1,128)S(1)}, u32[]{:S(2)}) copy-start(f32[1,512]{1,0:T(1,128)S(1)} %get-tuple-element.163) | copy-start | bytes 6148
  19.7 103.3 %copy-start.43 = (f32[1,512]{1,0:T(1,128)}, f32[1,512]{1,0:T(1,128)S(1)}, u32[]{:S(2)}) copy-start(f32[1,512]{1,0:T(1,128)S(1)} %get-tuple-element.164) | copy-start | bytes 6148
  19.8 103.2 %copy-start.35 = (f32[8,68]{1,0:T(8,128)}, f32[8,68]{1,0:T(8,128)S(1)}, u32[]{:S(2)}) copy-start(f32[8,68]{1,0:T(8,128)S(1)} %get-tuple-element.168) | copy-start | bytes 6532
  19.8 103.2 %copy-start.45 = (f32[8,68]{1,0:T(8,128)}, f32[8,68]{1,0:T(8,128)S(1)}, u32[]{:S(2)}) copy-start(f32[8,68]{1,0:T(8,128)S(1)} %get-tuple-element.165) | copy-start | bytes 6532
  19.8 103.2 %copy-start.47 = (f32[8,68]{1,0:T(8,128)}, f32[8,68]{1,0:T(8,128)S(1)}, u32[]{:S(2)}) copy-start(f32[8,68]{1,0:T(8,128)S(1)} %get-tuple-element.166) | copy-start | bytes 6532
  19.8 103.2 %copy-start.48 = (f32[8,68]{1,0:T(8,128)}, f32[8,68]{1,0:T(8,128)S(1)}, u32[]{:S(2)}) copy-start(f32[8,68]{1,0:T(8,128)S(1)} %get-tuple-element.167) | copy-start | bytes 6532
  33.0 91.3 %copy-start.27 = (bf16[512,32]{0,1:T(8,128)(2,1)}, bf16[512,32]{0,1:T(8,128)(2,1)S(1)}, u32[]{:S(2)}) copy-start(bf16[512,32]{0,1:T(8,128)(2,1)S(1)} %reshape.369) | copy-start | bytes 98308
  33.1 91.2 %copy-start.23 = (bf16[512,128]{0,1:T(8,128)(2,1)}, bf16[512,128]{0,1:T(8,128)(2,1)S(1)}, u32[]{:S(2)}) copy-start(bf16[512,128]{0,1:T(8,128)(2,1)S(1)} %copy.199) | copy-start | bytes 393220
  35.2 95.8 %copy-start.29 = (f32[2,8,128]{2,1,0:T(8,128)}, f32[2,8,128]{2,1,0:T(8,128)S(1)}, u32[]{:S(2)}) copy-start(f32[2,8,128]{2,1,0:T(8,128)S(1)} %exponential_negate_fusion) | copy-start | bytes 24580
  66.7 60.2 %all-to-all-start.4 = ((bf16[4,8,64,128]{3,2,1,0:T(8,128)(2,1)}), bf16[4,8,64,128]{3,2,1,0:T(8,128)(2,1)S(1)}, u32[]{:S(2)}, u32[]{:S(2)}) async-start(bf16[4,8,64,128]{3,2,1,0:T(8,128)(2,1)} %bitcast.168), calls=%async_computation.4 | async-start | bytes 1048576 | tf_op jit(solution)/shard_map/all_to_all | solution.py:261
  126.9 17.7 %all-to-all-start = ((f32[8,64,160]{2,1,0:T(8,128)}), f32[8,64,160]{2,1,0:T(8,128)}, u32[]{:S(2)}, u32[]{:S(2)}) async-start(f32[8,64,160]{2,1,0:T(8,128)} %fusion.60), calls=%async_computation | async-start | bytes 1048576 | tf_op jit(solution)/shard_map/all_to_all | solution.py:264
  144.6 60.8 %all-to-all-start.1 = ((bf16[4,8,64,2,128]{4,2,1,3,0:T(8,128)(2,1)}), bf16[4,8,64,2,128]{4,2,1,3,0:T(8,128)(2,1)}, u32[]{:S(2)}, u32[]{:S(2)}) async-start(bf16[4,8,64,2,128]{4,2,1,3,0:T(8,128)(2,1)} %maximum_bitcast_fusion), calls=%async_computation.1 | async-start | bytes 2097152 | tf_op jit(solution)/shard_map/all_to_all | solution.py:261
  285.2 13.1 %all-to-all-start.7 = ((bf16[4,8,64,128]{3,2,1,0:T(8,128)(2,1)}), bf16[4,8,64,128]{3,2,1,0:T(8,128)(2,1)}, u32[]{:S(2)}, u32[]{:S(2)}) async-start(bf16[4,8,64,128]{3,2,1,0:T(8,128)(2,1)} %bitcast.204), calls=%async_computation.7 | async-start | bytes 1048576 | tf_op jit(solution)/shard_map/all_to_all | solution.py:261
  298.3 13.4 %all-to-all-start.5 = ((bf16[4,8,68,128]{3,1,2,0:T(8,128)(2,1)}), bf16[4,8,68,128]{3,1,2,0:T(8,128)(2,1)}, u32[]{:S(2)}, u32[]{:S(2)}) async-start(bf16[4,8,68,128]{3,1,2,0:T(8,128)(2,1)} %maximum_bitcast_fusion.1), calls=%async_computation.5 | async-start | bytes 1114112 | tf_op jit(solution)/shard_map/all_to_all | solution.py:261
  311.7 31.7 %all-to-all-start.6 = ((bf16[32,68,160]{2,1,0:T(8,128)(2,1)}), bf16[32,68,160]{2,1,0:T(8,128)(2,1)S(1)}, u32[]{:S(2)}, u32[]{:S(2)}) async-start(bf16[32,68,160]{2,1,0:T(8,128)(2,1)} %pad_maximum_fusion), calls=%async_computation.6 | async-start | bytes 2359296 | tf_op jit(solution)/shard_map/all_to_all | solution.py:417
  323.6 51.2 %copy-start.46 = (f32[8,68]{1,0:T(8,128)S(1)}, f32[8,68]{1,0:T(8,128)}, u32[]{:S(2)}) copy-start(f32[8,68]{1,0:T(8,128)} %copy-done.45) | copy-start | bytes 6532
  384.6 46.2 %all-to-all-start.8 = ((bf16[8,64,2048]{2,1,0:T(8,128)(2,1)}), bf16[8,64,2048]{2,1,0:T(8,128)(2,1)}, u32[]{:S(2)}, u32[]{:S(2)}) async-start(bf16[8,64,2048]{2,1,0:T(8,128)(2,1)} %bitcast.199), calls=%async_computation.8 | async-start | bytes 4194304 | tf_op jit(solution)/shard_map/all_to_all | solution.py:264
  389.1 47.5 %all-gather.25.cloned.1.call-start = ((), (), s32[]{:S(2)}) async-start(), calls=%async_computation.13 | async-start | bytes 2621440 | tf_op jit(solution)/shard_map/all_gather | solution.py:258
  390.0 176.2 %all-reduce.13.cloned.1.call-start = ((), (), s32[]{:S(2)}) async-start(), calls=%async_computation.12 | async-start | bytes 655360 | tf_op jit(solution)/shard_map/psum | solution.py:480
  391.1 178.2 %all-gather.31.cloned.1.call-start = ((), (), s32[]{:S(2)}) async-start(), calls=%async_computation.16 | async-start | bytes 1310720 | tf_op jit(solution)/shard_map/all_gather | solution.py:258
  434.0 138.9 %all-gather.23.cloned.1.call-start = ((), (), s32[]{:S(2)}) async-start(), calls=%async_computation.11 | async-start | bytes 5242880 | tf_op jit(solution)/shard_map/all_gather | solution.py:258
  436.5 142.9 %all-gather.27.cloned.1.call-start = ((), (), s32[]{:S(2)}) async-start(), calls=%async_computation.14 | async-start | bytes 1310720 | tf_op jit(solution)/shard_map/all_gather | solution.py:258
  499.9 85.1 %all-gather.33.cloned.1.call-start = ((), (), s32[]{:S(2)}) async-start(), calls=%async_computation.17 | async-start | bytes 10485760 | tf_op jit(solution)/shard_map/all_gather | solution.py:258
  500.7 144.2 %all-gather.21.cloned.1.call-start = ((), (), s32[]{:S(2)}) async-start(), calls=%async_computation.10 | async-start | bytes 10485760 | tf_op jit(solution)/shard_map/all_gather | solution.py:258
  (45 other events, 380.9 us)
Sparse Core Ops, SparseCore 0:
  10.7 52.0 all-gather.28
  65.5 50.5 all-gather.18
  392.0 23.8 all-gather.24
  418.1 32.2 all-reduce.12
  451.9 16.7 all-gather.30
  470.6 34.4 all-gather.22
  507.3 17.0 all-gather.26
  525.9 59.0 all-gather.32
  586.6 58.2 all-gather.20
